TPU v7x, 128 devices: a whole 4x4x4 slice. The times are simulated.
128 devices in a mesh: row: 32 (over z_lo, y, x), col: 4 (over z_hi, core).
Axes of the slice: x: 4, y: 4, z: 4 (z_hi: 2, z_lo: 2; z = z_hi * 2 + z_lo), core: 2. Of those that a mesh axis runs over, the one named last changes fastest.
Arguments:
- panel_tiles: float32 [65536, 1024], P('row', 'col'), may hold values from -48 to 48
- left_u: bfloat16 [65536, 6144], P('row', 'col'), may hold values from -8 to 8
- earlier_right_factors: bfloat16 [65536, 6144], P('row', 'col'), may hold values from -0.25 to 0.25
- tile_global_index: int32 [64], replicated, may hold values from 0 to 63, as said below
Outputs:
- panel_factor: float32 [65536, 1024], P('row', 'col')
Inputs may be any that keep to these rules, and one draw needn't show every extreme that they name: `tile_global_index`: A permutation; slot pivot, the one numbered 0, holds the diagonal tile.
All inputs are finite; a program needn't handle non-finite values.
Results may differ from a plain program's by a relative error of at most 0.00053.
Values may be sent and summed in bfloat16 or wider, within the bound.
No kernel may reach another device: no remote copies, remote signals or barrier semaphores. Data moves between devices by JAX's collectives and lax.ppermute only.
A program may use at most 128 MiB of HBM per device.

v0:
```python
import jax
import jax.numpy as jnp
from jax import lax
from jax.sharding import Mesh
from jax.sharding import PartitionSpec as P

TILE = 1024
RANK = 256
TILE_DEV = 2
COL_DEV = 6
ROW = ("row_0", "row_1", "row_2")


def from_root(value, axis, source):
    kept = jnp.where(lax.axis_index(axis) == source, value, 0).astype(value.dtype)
    return lax.psum(kept, axis)


def split_up(value, dim, devices):
    shape = value.shape
    parts = value.reshape(*shape[:dim], devices, shape[dim] // devices, *shape[dim + 1 :])
    return jnp.moveaxis(parts, dim, 0)


def summed_on_arrival(value, axis, dim):
    devices = lax.axis_size(axis)
    parts = lax.all_to_all(split_up(value, dim, devices), axis, 0, 0, tiled=True)
    return jnp.sum(parts, axis=0)


def broadcast_by_axis(value, axes, root):
    value = jnp.where(lax.axis_index(axes) == root, value, jnp.zeros_like(value))
    for axis in axes:
        value = lax.psum(value, axis)
    return value


def local(panel_tiles, left_u, earlier_right_factors, tile_global_index):
    tile_count = tile_global_index.shape[0]
    pivot_position = jnp.sum(
        jnp.where(tile_global_index == 0, jnp.arange(tile_count, dtype=jnp.int32), 0)
    )
    owner_row = pivot_position // TILE_DEV
    local_slot = pivot_position % TILE_DEV
    my_row = lax.axis_index(ROW)
    my_col = lax.axis_index("col")
    col_width = panel_tiles.shape[1]
    pivot_left = lax.dynamic_slice_in_dim(left_u, local_slot * TILE, TILE, 0)
    pivot_right = lax.dynamic_slice_in_dim(earlier_right_factors, local_slot * TILE, TILE, 0)
    pivot_left, pivot_right = (
        from_root(pivot_left, ROW, owner_row),
        from_root(pivot_right, ROW, owner_row),
    )
    left_blocks = left_u.reshape(TILE_DEV, TILE, COL_DEV, RANK)
    right_blocks = earlier_right_factors.reshape(TILE_DEV, TILE, COL_DEV, RANK)
    pivot_triple = pivot_right.reshape(TILE, COL_DEV, RANK)
    inner_small = jnp.einsum(
        "tbjr,bjs->tjrs", right_blocks, pivot_triple, preferred_element_type=jnp.float32
    ).astype(jnp.bfloat16)
    left_small = jnp.einsum(
        "tbjr,tjrs->tbjs", left_blocks, inner_small, preferred_element_type=jnp.float32
    ).astype(jnp.bfloat16)
    update_terms = jnp.einsum(
        "nk,mk->nm",
        left_small.reshape(TILE_DEV * TILE, COL_DEV * RANK),
        pivot_left,
        preferred_element_type=jnp.float32,
    )
    own_sums = summed_on_arrival(update_terms, "col", 1)
    updated_tiles = lax.all_gather(panel_tiles - own_sums, "col", axis=1, tiled=True)
    diagonal = lax.dynamic_slice_in_dim(updated_tiles, local_slot * TILE, TILE, 0)
    identity = jnp.eye(TILE, dtype=jnp.float32)
    cholesky_factor = jnp.linalg.cholesky(diagonal)
    inverted_factor = lax.linalg.triangular_solve(
        cholesky_factor, identity, left_side=True, lower=True
    )
    rows_inv = lax.dynamic_slice_in_dim(inverted_factor, my_col * col_width, col_width, 0)
    rows_inv = broadcast_by_axis(rows_inv, ROW, owner_row)
    solved_rows = lax.dot_general(
        updated_tiles,
        rows_inv,
        (((1,), (1,)), ((), ())),
        precision=lax.Precision.HIGHEST,
        preferred_element_type=jnp.float32,
    )
    factor_cols = lax.dynamic_slice_in_dim(cholesky_factor, my_col * col_width, col_width, 1)
    row_tiles = jnp.arange(TILE_DEV * TILE, dtype=jnp.int32) // TILE
    chosen_rows = jnp.logical_and(my_row == owner_row, row_tiles == local_slot)
    return jnp.where(chosen_rows[:, None], jnp.tile(factor_cols, (TILE_DEV, 1)), solved_rows)


def solution(mesh):
    split = Mesh(
        mesh.devices.reshape(2, 4, 4, mesh.shape["col"]), ("row_0", "row_1", "row_2", "col")
    )
    return jax.shard_map(
        local,
        mesh=split,
        in_specs=(P(ROW, "col"), P(ROW, "col"), P(ROW, "col"), P()),
        out_specs=P(ROW, "col"),
        check_vma=False,
    )
```

profile of v0, /device:TPU:0, one launch (start us, length us, event | category | flops | bytes accessed | tf_op | source)
XLA Modules:
  0.0 1110.6 jit_solution(5675291476867327517)
XLA Ops:
  30.5 13.3 %reshape.130 = bf16[2,1024,6,256]{3,2,1,0:T(8,128)(2,1)} reshape(bf16[2048,1536]{1,0:T(8,128)(2,1)} %param.5) | data formatting | bytes 12582912 | tf_op jit(solution)/shard_map/reshape | solution.py:54
  43.8 13.4 %reshape.129 = bf16[2,1024,6,256]{3,2,1,0:T(8,128)(2,1)} reshape(bf16[2048,1536]{1,0:T(8,128)(2,1)} %param.6) | data formatting | bytes 12582912 | tf_op jit(solution)/shard_map/reshape | solution.py:55
  57.2 310.4 %all-reduce.13.cloned.1.call-done = (bf16[1024,6,256]{0,2,1:T(8,128)(2,1)}, bf16[4,256,1536]{2,1,0:T(8,128)(2,1)}) async-done(((bf16[1024,6,256]{0,2,1:T(8,128)(2,1)}, bf16[4,256,1536]{2,1,0:T(8,128)(2,1)}), (bf16[1024,6,256]{0,2,1:T(8,128)(2,1)}, bf16[4,256,1536]{2,1,0:T(8,128)(2,1)})) %all-reduce.13.cloned.1.call-update) | async-done | bytes 6291472 | tf_op jit(solution)/shard_map/psum | solution.py:16
  367.6 16.6 %convert_bitcast_fusion = bf16[2,1024,6,256]{1,3,2,0:T(8,128)(2,1)} fusion(bf16[2,1024,6,256]{3,2,1,0:T(8,128)(2,1)} %reshape.130, bf16[2,1024,6,256]{3,2,1,0:T(8,128)(2,1)} %reshape.129, bf16[1024,6,256]{0,2,1:T(8,128)(2,1)} %get-tuple-element.21), kind=kOutput, calls=%fused_computation.6 | convolution fusion | flops 3225157632 | bytes 22020096 | tf_op jit(solution)/shard_map/tbjr,tjrs->tbjs/dot_general | solution.py:60
  384.2 12.7 %copy.23 = bf16[2,1024,6,256]{1,0,3,2:T(2,128)(2,1)} copy(bf16[2,1024,6,256]{1,3,2,0:T(8,128)(2,1)} %convert_bitcast_fusion) | data formatting | bytes 12582912 | tf_op jit(solution)/shard_map/convert_element_type | solution.py:62
  396.8 11.3 %reshape.133 = bf16[2048,1536,1]{0,1,2:T(8,128)(2,1)} reshape(bf16[2,1024,6,256]{1,0,3,2:T(2,128)(2,1)} %copy.23) | data formatting | bytes 12582912 | tf_op jit(solution)/shard_map/reshape | solution.py:65
  408.2 11.0 convolution_bitcast_fusion
  426.8 92.7 %all-to-all-done = f32[4,2048,256]{2,1,0:T(8,128)} async-done(((f32[4,2048,256]{2,1,0:T(8,128)}), f32[4,2048,256]{2,1,0:T(8,128)}, u32[]{:S(2)}, u32[]{:S(2)}) %all-to-all-start) | async-done | bytes 8388640 | tf_op jit(solution)/shard_map/all_to_all | solution.py:27
  534.0 58.3 %all-gather.2.cloned.1.call-done = f32[2048,1024]{0,1:T(8,128)} async-done(((f32[2048,256]{0,1:T(8,128)}), f32[2048,1024]{0,1:T(8,128)}) %all-gather.2.cloned.1.call-update) | async-done | bytes 8388624 | tf_op jit(solution)/shard_map/all_gather | solution.py:70
  609.3 11.7 %cholesky.223 = f32[128,128]{1,0:T(8,128)S(1)} custom-call(f32[128,128]{1,0:T(8,128)S(1)} %cholesky.580), custom_call_target="Cholesky" | custom-call | tf_op jit(solution)/shard_map/jit(cholesky)/cholesky | solution.py:73
  637.3 11.9 %cholesky.244 = f32[128,128]{1,0:T(8,128)S(1)} custom-call(f32[128,128]{1,0:T(8,128)S(1)} %cholesky.584), custom_call_target="Cholesky" | custom-call | tf_op jit(solution)/shard_map/jit(cholesky)/cholesky | solution.py:73
  662.9 11.7 %cholesky.468 = f32[128,128]{1,0:T(8,128)S(1)} custom-call(f32[128,128]{1,0:T(8,128)S(1)} %cholesky.589), custom_call_target="Cholesky" | custom-call | tf_op jit(solution)/shard_map/jit(cholesky)/cholesky | solution.py:73
  688.6 11.9 %cholesky.487 = f32[128,128]{1,0:T(8,128)S(1)} custom-call(f32[128,128]{1,0:T(8,128)S(1)} %cholesky.594), custom_call_target="Cholesky" | custom-call | tf_op jit(solution)/shard_map/jit(cholesky)/cholesky | solution.py:73
  714.5 11.7 %cholesky.506 = f32[128,128]{1,0:T(8,128)S(1)} custom-call(f32[128,128]{1,0:T(8,128)S(1)} %cholesky.599), custom_call_target="Cholesky" | custom-call | tf_op jit(solution)/shard_map/jit(cholesky)/cholesky | solution.py:73
  726.8 10.2 custom-call.66
  740.3 11.7 %cholesky.526 = f32[128,128]{1,0:T(8,128)S(1)} custom-call(f32[128,128]{1,0:T(8,128)S(1)} %cholesky.604), custom_call_target="Cholesky" | custom-call | tf_op jit(solution)/shard_map/jit(cholesky)/cholesky | solution.py:73
  765.5 11.7 %cholesky.546 = f32[128,128]{1,0:T(8,128)S(1)} custom-call(f32[128,128]{1,0:T(8,128)S(1)} %cholesky.609), custom_call_target="Cholesky" | custom-call | tf_op jit(solution)/shard_map/jit(cholesky)/cholesky | solution.py:73
  790.3 11.7 %cholesky.564 = f32[128,128]{1,0:T(8,128)S(1)} custom-call(f32[128,128]{1,0:T(8,128)S(1)} %convolution_subtract_fusion.11), custom_call_target="Cholesky" | custom-call | tf_op jit(solution)/shard_map/jit(cholesky)/cholesky | solution.py:73
  817.1 23.1 %while.1 = (s32[]{:T(128)}, f32[1024,1024]{1,0:T(8,128)}, s32[8,2]{0,1:T(2,128)S(1)}, f32[8,128,128]{2,1,0:T(8,128)S(1)}, s32[]{:T(128)}) while((s32[]{:T(128)}, f32[1024,1024]{1,0:T(8,128)}, s32[8,2]{0,1:T(2,128)S(1)}, f32[8,128,128]{2,1,0:T(8,128)S(1)}, s32[]{:T(128)}) %tuple.58), condition=%wide.while_cond, body=%wide.while_body.sunk | while | flops 2 | bytes 131189 | solution.py:74
  840.2 78.8 %custom-call.69 = f32[8,128,128]{1,2,0:T(8,128)S(1)} custom-call(f32[8,128,128]{2,1,0:T(8,128)S(1)} %get-tuple-element.12), custom_call_target="InvertDiagBlocksLowerTriangular" | custom-call | tf_op jit(solution)/shard_map/triangular_solve | solution.py:74
  942.5 46.1 %all-reduce.7.cloned.1.call-done = f32[256,1024]{1,0:T(8,128)} async-done(((f32[256,1024]{1,0:T(8,128)}), f32[256,1024]{1,0:T(8,128)}) %all-reduce.7.cloned.1.call-update) | async-done | bytes 1048592 | tf_op jit(solution)/shard_map/psum | solution.py:34
  988.6 49.1 %all-reduce.9.cloned.1.call-done = f32[256,1024]{1,0:T(8,128)} async-done(((f32[256,1024]{1,0:T(8,128)}), f32[256,1024]{1,0:T(8,128)}) %all-reduce.9.cloned.1.call-update) | async-done | bytes 1048592 | tf_op jit(solution)/shard_map/psum | solution.py:34
  1039.0 47.5 %all-reduce.11.cloned.1.call-done = f32[256,1024]{1,0:T(8,128)} async-done(((f32[256,1024]{1,0:T(8,128)}), f32[256,1024]{1,0:T(8,128)}) %all-reduce.11.cloned.1.call-update) | async-done | bytes 1048592 | tf_op jit(solution)/shard_map/psum | solution.py:34
  1086.7 17.0 %convolution_select_fusion = f32[2048,256]{1,0:T(8,128)} fusion(f32[2048,256]{1,0:T(8,128)S(1)} %bitcast.126, f32[2048,1024]{0,1:T(8,128)} %all-gather.2.cloned.1.call-done, f32[256,1024]{1,0:T(8,128)} %all-reduce.11.cloned.1.call-done, pred[2048]{0:T(1024)(128)(4,1)S(1)} %fusion.93), kind=kOutput, calls=%fused_computation.17 | convolution fusion | flops 6442975232 | bytes 13633536 | tf_op jit(solution)/shard_map/dot_general | solution.py:79
  (126 shorter events, 206.7 us)
Async XLA Ops:
  6.5 361.0 %all-reduce.13.cloned.1.call-start = ((), (), s32[]{:S(2)}) async-start(), calls=%async_computation.5 | async-start | bytes 12582912 | tf_op jit(solution)/shard_map/psum | solution.py:16
  24.3 3.0 copy-start.1
  396.8 11.3 %copy-start.3 = (bf16[4,256,1536]{2,1,0:T(8,128)(2,1)S(1)}, bf16[4,256,1536]{2,1,0:T(8,128)(2,1)}, u32[]{:S(2)}) copy-start(bf16[4,256,1536]{2,1,0:T(8,128)(2,1)} %get-tuple-element.22) | copy-start | bytes 9437188
  419.1 100.4 %all-to-all-start = ((f32[4,2048,256]{2,1,0:T(8,128)}), f32[4,2048,256]{2,1,0:T(8,128)}, u32[]{:S(2)}, u32[]{:S(2)}) async-start(f32[4,2048,256]{2,1,0:T(8,128)} %convolution_bitcast_fusion), calls=%async_computation | async-start | bytes 16777216 | tf_op jit(solution)/shard_map/all_to_all | solution.py:27
  424.8 167.6 %all-gather.2.cloned.1.call-start = ((), (), s32[]{:S(2)}) async-start(), calls=%async_computation.1 | async-start | bytes 10485760 | tf_op jit(solution)/shard_map/all_gather | solution.py:70
  531.2 457.4 %all-reduce.7.cloned.1.call-start = ((), (), s32[]{:S(2)}) async-start(), calls=%async_computation.2 | async-start | bytes 2097152 | tf_op jit(solution)/shard_map/psum | solution.py:34
  607.3 2.0 copy-start.2
  919.0 3.2 copy-start
  942.4 95.3 %all-reduce.9.cloned.1.call-start = ((), (), s32[]{:S(2)}) async-start(), calls=%async_computation.3 | async-start | bytes 2097152 | tf_op jit(solution)/shard_map/psum | solution.py:34
  988.6 97.9 %all-reduce.11.cloned.1.call-start = ((), (), s32[]{:S(2)}) async-start(), calls=%async_computation.4 | async-start | bytes 2097152 | tf_op jit(solution)/shard_map/psum | solution.py:34
Sparse Core Ops, SparseCore 0:
  30.6 336.8 all-reduce.12
  531.3 61.0 all-gather.1
  942.6 45.9 all-reduce.6
  990.9 46.7 all-reduce.8
  1039.9 46.5 all-reduce.10
where the time goes:
time: 1120 us; the launch traced here: 1110 us
  waiting for transfers between devices  604 us (54%)
  other arithmetic  276 us (25%)
  local copies, waits for them, and re-layouts  113 us (10%)
  matrix products  89.8 us (8%)
  between operations  21.5 us (2%)
    psum x1, waiting for transfers between devices, from_root(): return lax.psum(kept, axis)  310 us
    another operation x31, other arithmetic, local(): cholesky_factor = jnp.linalg.cholesky(diagonal)  173 us
    psum x3, waiting for transfers between devices, broadcast_by_axis(): value = lax.psum(value, axis)  143 us
    all_to_all x1, waiting for transfers between devices, summed_on_arrival(): lax.all_to_all(split_up(value, dim, devices), axis, 0, 0, tiled=True)  92.7 us
    another operation x3, other arithmetic, local(): lax.linalg.triangular_solve(cholesky_factor, identity, left_side=True, lo...  83.2 us
    all_gather x1, waiting for transfers between devices, local(): lax.all_gather(panel_tiles - own_sums, 'col', axis=1, tiled=True)  58.3 us
    another operation x14, matrix products, local(): cholesky_factor = jnp.linalg.cholesky(diagonal)  23.1 us
    another operation x24, local copies, waits for them, and re-layouts  23 us
  transfers between devices with their start and end apart: 6, of which 6 were waited for; matrix products, arithmetic and copies ran while one was open for 3% of the time, Pallas kernels for 0%

commit v1 on v0

v1 whole, which is shorter than its diff:
```python
import jax
import jax.numpy as jnp
from jax import lax
from jax.sharding import Mesh
from jax.sharding import PartitionSpec as P

TILE = 1024
RANK = 256
TILE_DEV = 2
COL_DEV = 6
BLOCK = 256
ROW = ("zl", "y", "x")
COL = ("zh", "core")
LOWER = ((0, 0), (1, 1), (2, 2), (1, 0), (2, 0), (3, 3), (2, 1), (3, 2), (3, 1), (3, 0))


def shift(value, axis, step):
    devices = lax.axis_size(axis)
    return lax.ppermute(value, axis, [(i, (i + step) % devices) for i in range(devices)])


def scatter(value, axis, away):
    quarter = value.shape[0] // 4
    parts = [value[k * quarter : (k + 1) * quarter] for k in range(4)]
    got = [parts[0]] + [shift(parts[k], axis, k) for k in (1, 2, 3)]
    return lax.select_n(away, *got)


def gather(piece, axis, away):
    quarter = piece.shape[0]
    got = [piece] + [shift(piece, axis, k) for k in (1, 2, 3)]
    whole = jnp.zeros((4 * quarter, *piece.shape[1:]), piece.dtype)
    for k in range(4):
        whole = lax.dynamic_update_slice_in_dim(whole, got[k], (away - k) % 4 * quarter, 0)
    return whole


def from_root(value, first, second, away):
    piece = scatter(value, first, away[first])
    piece = scatter(piece, second, away[second])
    piece = jnp.where(away["zl"] == 0, piece, shift(piece, "zl", 1))
    piece = gather(piece, second, away[second])
    return gather(piece, first, away[first])


def low_rank(left, right, pivot_right):
    rows = left.shape[0] // TILE
    left = left.reshape(rows, TILE, COL_DEV, RANK)
    right = right.reshape(rows, TILE, COL_DEV, RANK)
    pivot_right = pivot_right.reshape(TILE, COL_DEV, RANK)
    inner = jnp.einsum(
        "tbjr,bjs->tjrs", right, pivot_right, preferred_element_type=jnp.float32
    ).astype(jnp.bfloat16)
    product = jnp.einsum(
        "tbjr,tjrs->tbjs", left, inner, preferred_element_type=jnp.float32
    ).astype(jnp.bfloat16)
    return product.reshape(rows * TILE, COL_DEV * RANK)


def times_transposed(a, b):
    return lax.dot_general(a, b, (((1,), (1,)), ((), ())), preferred_element_type=jnp.float32)


def local(panel_tiles, left_u, earlier_right_factors, tile_global_index):
    tile_count = tile_global_index.shape[0]
    pivot_position = jnp.sum(
        jnp.where(tile_global_index == 0, jnp.arange(tile_count, dtype=jnp.int32), 0)
    )
    owner = pivot_position // TILE_DEV
    slot = pivot_position % TILE_DEV
    away = {
        "x": (lax.axis_index("x") - owner % 4) % 4,
        "y": (lax.axis_index("y") - owner // 4 % 4) % 4,
        "zl": (lax.axis_index("zl") - owner // 16) % 2,
    }
    zh, core = lax.axis_index("zh"), lax.axis_index("core")
    my_col = lax.axis_index(COL)

    own_left = lax.dynamic_slice_in_dim(left_u, slot * TILE, TILE, 0)
    own_right = lax.dynamic_slice_in_dim(earlier_right_factors, slot * TILE, TILE, 0)
    own_panel = lax.dynamic_slice_in_dim(panel_tiles, slot * TILE, TILE, 0)
    pivot_right = from_root(own_right, "x", "y", away)
    pivot_left = from_root(own_left, "y", "x", away)

    term = -times_transposed(low_rank(own_left, own_right, own_right), own_left)
    mine = lax.dynamic_slice_in_dim(term, my_col * BLOCK, BLOCK, 1) + own_panel
    term = lax.dynamic_update_slice_in_dim(term, mine, my_col * BLOCK, 1)
    grid = term.reshape(4, BLOCK, 4, BLOCK)
    lower = jnp.stack([(grid[i, :, j] + grid[j, :, i].T) * 0.5 for i, j in LOWER])
    theirs = lax.dynamic_slice_in_dim(lower, (1 - core) * 5, 5, 0)
    part = lax.dynamic_slice_in_dim(lower, core * 5, 5, 0) + shift(theirs, "core", 1)
    part = (part + shift(part, "zh", 1)).reshape(5 * BLOCK, BLOCK)
    half = 5 * BLOCK // 2
    part = jnp.concatenate(
        [from_root(part[:half], "x", "y", away), from_root(part[half:], "y", "x", away)]
    ).reshape(5, BLOCK, BLOCK)
    other = shift(part, "core", 1)
    parts = jnp.concatenate(
        [jnp.where(core == 0, part, other), jnp.where(core == 0, other, part)]
    )
    rows = []
    for i in range(4):
        rows.append(
            jnp.concatenate(
                [parts[LOWER.index((max(i, j), min(i, j)))] for j in range(4)], axis=1
            )
        )
    diagonal = jnp.concatenate(rows, axis=0)

    product = low_rank(left_u, earlier_right_factors, pivot_right)

    def for_column(z, c):
        block = lax.dynamic_slice_in_dim(pivot_left, (2 * z + c) * BLOCK, BLOCK, 0)
        return times_transposed(product, block)

    far = for_column(1 - zh, core) + shift(for_column(1 - zh, 1 - core), "core", 1)
    near = for_column(zh, core) + shift(for_column(zh, 1 - core), "core", 1)
    updated = panel_tiles - near - shift(far, "zh", 1)
    updated_z = shift(updated, "zh", 1)
    updated_c = shift(updated, "core", 1)
    updated_zc = shift(updated_z, "core", 1)

    factor = lax.linalg.cholesky(diagonal, symmetrize_input=False)
    inverse = lax.linalg.triangular_solve(
        factor, jnp.eye(TILE, dtype=jnp.float32), left_side=True, lower=True
    )
    rows_inv = lax.dynamic_slice_in_dim(inverse, my_col * BLOCK, BLOCK, 0)

    def solved_part(block, z, c):
        return lax.dot_general(
            block,
            lax.dynamic_slice_in_dim(rows_inv, (2 * z + c) * BLOCK, BLOCK, 1),
            (((1,), (1,)), ((), ())),
            precision=lax.Precision.HIGHEST,
            preferred_element_type=jnp.float32,
        )

    solved = solved_part(updated, zh, core) + solved_part(updated_z, 1 - zh, core)
    solved = solved + solved_part(updated_c, zh, 1 - core)
    solved = solved + solved_part(updated_zc, 1 - zh, 1 - core)
    factor_cols = lax.dynamic_slice_in_dim(factor, my_col * BLOCK, BLOCK, 1)
    row_tiles = jnp.arange(TILE_DEV * TILE, dtype=jnp.int32) // TILE
    chosen = jnp.logical_and(lax.axis_index(ROW) == owner, row_tiles == slot)
    return jnp.where(chosen[:, None], jnp.tile(factor_cols, (TILE_DEV, 1)), solved)


def solution(mesh):
    split = Mesh(mesh.devices.reshape(2, 4, 4, 2, 2), ("zl", "y", "x", "zh", "core"))
    return jax.shard_map(
        local,
        mesh=split,
        in_specs=(P(ROW, COL), P(ROW, COL), P(ROW, COL), P()),
        out_specs=P(ROW, COL),
        check_vma=False,
    )
```

time: 1120 us -> 807 us (0.72)
  waiting for transfers between devices: 604 us -> 117 us
  starting transfers between devices: 5.86 us -> 86.1 us
  local copies, waits for them, and re-layouts: 113 us -> 180 us
  other arithmetic: 276 us -> 296 us
  matrix products: 89.8 us -> 106 us
  between operations: 21.5 us -> 9.11 us
    psum x4 -> x0, waiting for transfers between devices: 453 us -> none  [the longest x1 310 us: from_root(): return lax.psum(kept, axis)]
    ppermute x0 -> x61, waiting for transfers between devices: none -> 117 us  [shift(): lax.ppermute(value, axis, [(i, (i + step) % devices) for i in range(devic...]
    all_to_all x1 -> x0, waiting for transfers between devices: 92.7 us -> none  [summed_on_arrival(): lax.all_to_all(split_up(value, dim, devices), axis, 0, 0, tiled=True)]
    ppermute x0 -> x61, starting transfers between devices: none -> 86.1 us  [shift(): lax.ppermute(value, axis, [(i, (i + step) % devices) for i in range(devic...]
    all_gather x1 -> x0, waiting for transfers between devices: 58.3 us -> none  [local(): lax.all_gather(panel_tiles - own_sums, 'col', axis=1, tiled=True)]
    dynamic_update_slice x0 -> x30, local copies, waits for them, and re-layouts: none -> 42.5 us  [gather(): lax.dynamic_update_slice_in_dim(whole, got[k], (away - k) % 4 * quarter, 0)]
    dot_general x3 -> x11, matrix products: 44.5 us -> 62 us  [the longest x5 30.6 us: times_transposed(): lax.dot_general(a, b, (((1,), (1,)), ((), ())), preferred_element_type=jn...]
    slice x0 -> x8, local copies, waits for them, and re-layouts: none -> 16.9 us  [the longest x1 12 us: local(): grid[i, :, j] + grid[j, :, i].T]
  transfers between devices with their start and end apart: 6 -> 61, of which waited for: 6 -> 23; matrix products, arithmetic and copies ran while one was open for 3% -> 62% of each run, Pallas kernels for 0% -> 0%
where the time goes in v1:
time: 807 us; the launch traced here: 793 us
  other arithmetic  296 us (37%)
  local copies, waits for them, and re-layouts  180 us (22%)
  waiting for transfers between devices  117 us (14%)
  matrix products  106 us (13%)
  starting transfers between devices  86.1 us (11%)
  between operations  9.11 us (1%)
    another operation x31, other arithmetic, local(): factor = lax.linalg.cholesky(diagonal, symmetrize_input=False)  173 us
    ppermute x61, waiting for transfers between devices, shift(): lax.ppermute(value, axis, [(i, (i + step) % devices) for i in range(devic...  117 us
    another operation x3, other arithmetic, local(): lax.linalg.triangular_solve(factor, jnp.eye(TILE, dtype=jnp.float32), lef...  86.1 us
    ppermute x61, starting transfers between devices, shift(): lax.ppermute(value, axis, [(i, (i + step) % devices) for i in range(devic...  86.1 us
    dynamic_update_slice x30, local copies, waits for them, and re-layouts, gather(): lax.dynamic_update_slice_in_dim(whole, got[k], (away - k) % 4 * quarter, 0)  42.5 us
    another operation x32, local copies, waits for them, and re-layouts  33.1 us
    dot_general x5, matrix products, times_transposed(): lax.dot_general(a, b, (((1,), (1,)), ((), ())), preferred_element_type=jn...  30.6 us
    unnamed x36, local copies, waits for them, and re-layouts  24.9 us
  transfers between devices with their start and end apart: 61, of which 23 were waited for; matrix products, arithmetic and copies ran while one was open for 62% of the time, Pallas kernels for 0%

profile of v1, /device:TPU:0, one launch (start us, length us, event | category | flops | bytes accessed | tf_op | source)
XLA Modules:
  0.0 792.9 jit_solution(2119705416995581328)
XLA Ops:
  36.9 12.0 %fusion.170 = (f32[1,256,1,256]{3,2,1,0:T(1,128)}, f32[1,256,1,256]{3,2,1,0:T(1,128)}, f32[1,256,1,256]{3,2,1,0:T(1,128)}, f32[1,256,1,256]{3,2,1,0:T(1,128)}, f...) fusion(f32[4,256,4,256]{3,2,1,0:T(4,128)} %reshape.124), kind=kLoop, calls=%fused_computation.355 | loop fusion | bytes 8388608 | tf_op jit(solution)/shard_map/slice | solution.py:89
  96.9 13.3 %reshape.156 = bf16[2,1024,6,256]{3,2,1,0:T(8,128)(2,1)} reshape(bf16[2048,1536]{1,0:T(8,128)(2,1)} %param.5) | data formatting | bytes 12582912 | tf_op jit(solution)/shard_map/reshape | solution.py:48
  110.2 13.3 %reshape.155 = bf16[2,1024,6,256]{3,2,1,0:T(8,128)(2,1)} reshape(bf16[2048,1536]{1,0:T(8,128)(2,1)} %param.6) | data formatting | bytes 12582912 | tf_op jit(solution)/shard_map/reshape | solution.py:49
  134.8 14.6 %collective-permute-done.43 = bf16[256,1536]{0,1:T(8,128)(2,1)S(1)} collective-permute-done((bf16[256,1536]{0,1:T(8,128)(2,1)S(1)}, bf16[256,1536]{0,1:T(8,128)(2,1)S(1)}, u32[]{:S(2)}, u32[]{:S(2)}) %collective-permute-start.43) | collective-permute-done | bytes 786464 | tf_op jit(solution)/shard_map/ppermute | solution.py:19
  151.1 14.2 %collective-permute-done.44 = bf16[256,1536]{0,1:T(8,128)(2,1)S(1)} collective-permute-done((bf16[256,1536]{0,1:T(8,128)(2,1)S(1)}, bf16[256,1536]{0,1:T(8,128)(2,1)S(1)}, u32[]{:S(2)}, u32[]{:S(2)}) %collective-permute-start.44) | collective-permute-done | bytes 786464 | tf_op jit(solution)/shard_map/ppermute | solution.py:19
  170.5 10.1 %collective-permute-done.34 = bf16[64,1536]{0,1:T(8,128)(2,1)S(1)} collective-permute-done((bf16[64,1536]{0,1:T(8,128)(2,1)S(1)}, bf16[64,1536]{0,1:T(8,128)(2,1)S(1)}, u32[]{:S(2)}, u32[]{:S(2)}) %collective-permute-start.34) | collective-permute-done | bytes 196640 | tf_op jit(solution)/shard_map/ppermute | solution.py:19
  263.8 16.6 %convert_bitcast_fusion = bf16[2,1024,6,256]{1,3,2,0:T(8,128)(2,1)} fusion(bf16[2,1024,6,256]{3,2,1,0:T(8,128)(2,1)} %reshape.156, bf16[1024,6,256,1]{0,2,1,3:T(8,128)(2,1)} %bitcast.71, bf16[2,1024,6,256]{3,2,1,0:T(8,128)(2,1)} %reshape.155), kind=kOutput, calls=%fused_computation.6 | convolution fusion | flops 3225157632 | bytes 22020096 | tf_op jit(solution)/shard_map/tbjr,tjrs->tbjs/dot_general | solution.py:54
  313.1 14.1 %copy.54 = bf16[2,1024,6,256]{1,0,3,2:T(2,128)(2,1)S(1)} copy(bf16[2,1024,6,256]{1,3,2,0:T(8,128)(2,1)S(1)} %bitcast.351) | data formatting | bytes 12582912 | tf_op jit(solution)/shard_map/convert_element_type | solution.py:56
  400.6 11.7 %cholesky.223 = f32[128,128]{1,0:T(8,128)S(1)} custom-call(f32[128,128]{1,0:T(8,128)S(1)} %cholesky.580), custom_call_target="Cholesky" | custom-call | tf_op jit(solution)/shard_map/cholesky | solution.py:123
  414.8 9.8 %custom-call.47 = f32[1,128,128]{1,2,0:T(8,128)S(1)} custom-call(f32[1,128,128]{2,1,0:T(8,128)S(1)} %get-tuple-element.128), custom_call_target="InvertDiagBlocksLowerTriangular" | custom-call | tf_op jit(solution)/shard_map/cholesky | solution.py:123
  426.5 11.7 %cholesky.244 = f32[128,128]{1,0:T(8,128)S(1)} custom-call(f32[128,128]{1,0:T(8,128)S(1)} %cholesky.582), custom_call_target="Cholesky" | custom-call | tf_op jit(solution)/shard_map/cholesky | solution.py:123
  438.9 10.0 %custom-call.48 = f32[1,128,128]{1,2,0:T(8,128)S(1)} custom-call(f32[1,128,128]{2,1,0:T(8,128)S(1)} %get-tuple-element.125), custom_call_target="InvertDiagBlocksLowerTriangular" | custom-call | tf_op jit(solution)/shard_map/cholesky | solution.py:123
  452.1 11.7 %cholesky.468 = f32[128,128]{1,0:T(8,128)S(1)} custom-call(f32[128,128]{1,0:T(8,128)S(1)} %cholesky.586), custom_call_target="Cholesky" | custom-call | tf_op jit(solution)/shard_map/cholesky | solution.py:123
  464.5 9.8 %custom-call.49 = f32[1,128,128]{1,2,0:T(8,128)S(1)} custom-call(f32[1,128,128]{2,1,0:T(8,128)S(1)} %get-tuple-element.122), custom_call_target="InvertDiagBlocksLowerTriangular" | custom-call | tf_op jit(solution)/shard_map/cholesky | solution.py:123
  477.7 12.1 %cholesky.487 = f32[128,128]{1,0:T(8,128)S(1)} custom-call(f32[128,128]{1,0:T(8,128)S(1)} %cholesky.590), custom_call_target="Cholesky" | custom-call | tf_op jit(solution)/shard_map/cholesky | solution.py:123
  490.4 9.8 %custom-call.50 = f32[1,128,128]{1,2,0:T(8,128)S(1)} custom-call(f32[1,128,128]{2,1,0:T(8,128)S(1)} %get-tuple-element.119), custom_call_target="InvertDiagBlocksLowerTriangular" | custom-call | tf_op jit(solution)/shard_map/cholesky | solution.py:123
  503.6 11.7 %cholesky.506 = f32[128,128]{1,0:T(8,128)S(1)} custom-call(f32[128,128]{1,0:T(8,128)S(1)} %cholesky.594), custom_call_target="Cholesky" | custom-call | tf_op jit(solution)/shard_map/cholesky | solution.py:123
  529.2 11.7 %cholesky.526 = f32[128,128]{1,0:T(8,128)S(1)} custom-call(f32[128,128]{1,0:T(8,128)S(1)} %cholesky.598), custom_call_target="Cholesky" | custom-call | tf_op jit(solution)/shard_map/cholesky | solution.py:123
  554.3 11.7 %cholesky.546 = f32[128,128]{1,0:T(8,128)S(1)} custom-call(f32[128,128]{1,0:T(8,128)S(1)} %cholesky.603), custom_call_target="Cholesky" | custom-call | tf_op jit(solution)/shard_map/cholesky | solution.py:123
  566.7 10.0 %custom-call.53 = f32[1,128,128]{1,2,0:T(8,128)S(1)} custom-call(f32[1,128,128]{2,1,0:T(8,128)S(1)} %get-tuple-element.110), custom_call_target="InvertDiagBlocksLowerTriangular" | custom-call | tf_op jit(solution)/shard_map/cholesky | solution.py:123
  579.5 11.7 %cholesky.564 = f32[128,128]{1,0:T(8,128)S(1)} custom-call(f32[128,128]{1,0:T(8,128)S(1)} %slice_subtract_fusion.1), custom_call_target="Cholesky" | custom-call | tf_op jit(solution)/shard_map/cholesky | solution.py:123
  608.6 28.3 %while.1 = (s32[]{:T(128)}, f32[1024,1024]{1,0:T(8,128)}, s32[8,2]{0,1:T(2,128)S(1)}, f32[8,128,128]{2,1,0:T(8,128)}, s32[]{:T(128)}) while((s32[]{:T(128)}, f32[1024,1024]{1,0:T(8,128)}, s32[8,2]{0,1:T(2,128)S(1)}, f32[8,128,128]{2,1,0:T(8,128)}, s32[]{:T(128)}) %tuple.101), condition=%wide.while_cond, body=%wide.while_body.sunk | while | flops 2 | bytes 132205 | solution.py:124
  636.9 79.4 %custom-call.54 = f32[8,128,128]{1,2,0:T(8,128)S(1)} custom-call(f32[8,128,128]{2,1,0:T(8,128)} %get-tuple-element.12), custom_call_target="InvertDiagBlocksLowerTriangular" | custom-call | tf_op jit(solution)/shard_map/triangular_solve | solution.py:124
  741.4 35.9 %collective-permute-done.58 = f32[2048,256]{1,0:T(8,128)S(1)} collective-permute-done((f32[2048,256]{1,0:T(8,128)S(1)}, f32[2048,256]{1,0:T(8,128)S(1)}, u32[]{:S(2)}, u32[]{:S(2)}) %collective-permute-start.58) | collective-permute-done | bytes 2097184 | tf_op jit(solution)/shard_map/ppermute | solution.py:19
  (336 shorter events, 416.5 us)
Async XLA Ops:
  85.2 134.5 %collective-permute-start = (f32[5,256,256]{1,2,0:T(8,128)}, f32[5,256,256]{1,2,0:T(8,128)}, u32[]{:S(2)}, u32[]{:S(2)}) collective-permute-start(f32[5,256,256]{1,2,0:T(8,128)} %constant_dynamic-slice_fusion.2), channel_id=1, source_target_pairs={{0,1},{1,0},{2,3},{3,2},{4,5},{5,4},{6,7},{7,6},{8,9},{9,8},{10,11... | collective-permute-start | bytes 3932168 | tf_op jit(solution)/shard_map/ppermute | solution.py:19
  86.8 40.6 %collective-permute-start.29 = (bf16[256,1536]{0,1:T(8,128)(2,1)}, bf16[256,1536]{0,1:T(8,128)(2,1)}, u32[]{:S(2)}, u32[]{:S(2)}) collective-permute-start(bf16[256,1536]{0,1:T(8,128)(2,1)} %get-tuple-element.50), channel_id=1, source_target_pairs={{0,4},{4,8},{8,12},{12,0},{1,5},{5,9},{9,13},{13,1},{2,6},{6,10},{... | collective-permute-start | bytes 2359304 | tf_op jit(solution)/shard_map/ppermute | solution.py:19
  88.6 41.7 %collective-permute-start.30 = (bf16[256,1536]{0,1:T(8,128)(2,1)}, bf16[256,1536]{0,1:T(8,128)(2,1)}, u32[]{:S(2)}, u32[]{:S(2)}) collective-permute-start(bf16[256,1536]{0,1:T(8,128)(2,1)} %get-tuple-element.49), channel_id=1, source_target_pairs={{0,8},{4,12},{8,0},{12,4},{1,9},{5,13},{9,1},{13,5},{2,10},{6,14},... | collective-permute-start | bytes 2359304 | tf_op jit(solution)/shard_map/ppermute | solution.py:19
  91.3 40.3 %collective-permute-start.31 = (bf16[256,1536]{0,1:T(8,128)(2,1)}, bf16[256,1536]{0,1:T(8,128)(2,1)}, u32[]{:S(2)}, u32[]{:S(2)}) collective-permute-start(bf16[256,1536]{0,1:T(8,128)(2,1)} %get-tuple-element.48), channel_id=1, source_target_pairs={{0,12},{4,0},{8,4},{12,8},{1,13},{5,1},{9,5},{13,9},{2,14},{6,2},{... | collective-permute-start | bytes 2359304 | tf_op jit(solution)/shard_map/ppermute | solution.py:19
  94.3 39.8 %collective-permute-start.42 = (bf16[256,1536]{0,1:T(8,128)(2,1)}, bf16[256,1536]{0,1:T(8,128)(2,1)}, u32[]{:S(2)}, u32[]{:S(2)}) collective-permute-start(bf16[256,1536]{0,1:T(8,128)(2,1)} %get-tuple-element.47), channel_id=1, source_target_pairs={{0,16},{16,32},{32,48},{48,0},{1,17},{17,33},{33,49},{49,1},{2,18}... | collective-permute-start | bytes 2359304 | tf_op jit(solution)/shard_map/ppermute | solution.py:19
  130.3 35.0 %collective-permute-start.44 = (bf16[256,1536]{0,1:T(8,128)(2,1)S(1)}, bf16[256,1536]{0,1:T(8,128)(2,1)S(1)}, u32[]{:S(2)}, u32[]{:S(2)}) collective-permute-start(bf16[256,1536]{0,1:T(8,128)(2,1)S(1)} %copy-done.7), channel_id=1, source_target_pairs={{0,48},{16,0},{32,16},{48,32},{1,49},{17,1},{33,17},{49,33},{2,50}... | collective-permute-start | bytes 2359304 | tf_op jit(solution)/shard_map/ppermute | solution.py:19
  133.3 34.5 %collective-permute-start.32 = (bf16[64,1536]{0,1:T(8,128)(2,1)S(1)}, bf16[64,1536]{0,1:T(8,128)(2,1)S(1)}, u32[]{:S(2)}, u32[]{:S(2)}) collective-permute-start(bf16[64,1536]{0,1:T(8,128)(2,1)S(1)} %get-tuple-element.75), channel_id=1, source_target_pairs={{0,16},{16,32},{32,48},{48,0},{1,17},{17,33},{33,49},{49,1},{2,18}... | collective-permute-start | bytes 589832 | tf_op jit(solution)/shard_map/ppermute | solution.py:19
  134.0 34.6 %collective-permute-start.33 = (bf16[64,1536]{0,1:T(8,128)(2,1)S(1)}, bf16[64,1536]{0,1:T(8,128)(2,1)S(1)}, u32[]{:S(2)}, u32[]{:S(2)}) collective-permute-start(bf16[64,1536]{0,1:T(8,128)(2,1)S(1)} %get-tuple-element.74), channel_id=1, source_target_pairs={{0,32},{16,48},{32,0},{48,16},{1,33},{17,49},{33,1},{49,17},{2,34}... | collective-permute-start | bytes 589832 | tf_op jit(solution)/shard_map/ppermute | solution.py:19
  149.4 31.2 %collective-permute-start.34 = (bf16[64,1536]{0,1:T(8,128)(2,1)S(1)}, bf16[64,1536]{0,1:T(8,128)(2,1)S(1)}, u32[]{:S(2)}, u32[]{:S(2)}) collective-permute-start(bf16[64,1536]{0,1:T(8,128)(2,1)S(1)} %get-tuple-element.73), channel_id=1, source_target_pairs={{0,48},{16,0},{32,16},{48,32},{1,49},{17,1},{33,17},{49,33},{2,50}... | collective-permute-start | bytes 589832 | tf_op jit(solution)/shard_map/ppermute | solution.py:19
  199.3 23.3 %collective-permute-start.49 = (bf16[64,1536]{0,1:T(8,128)(2,1)S(1)}, bf16[64,1536]{0,1:T(8,128)(2,1)}, u32[]{:S(2)}, u32[]{:S(2)}) collective-permute-start(bf16[64,1536]{0,1:T(8,128)(2,1)S(1)} %broadcast_select_fusion.2), channel_id=1, source_target_pairs={{0,4},{4,8},{8,12},{12,0},{1,5},{5,9},{9,13},{13,1},{2,6},{6,10},{... | collective-permute-start | bytes 589832 | tf_op jit(solution)/shard_map/ppermute | solution.py:19
  212.9 24.2 %collective-permute-start.51 = (bf16[64,1536]{0,1:T(8,128)(2,1)S(1)}, bf16[64,1536]{0,1:T(8,128)(2,1)}, u32[]{:S(2)}, u32[]{:S(2)}) collective-permute-start(bf16[64,1536]{0,1:T(8,128)(2,1)S(1)} %broadcast_select_fusion.2), channel_id=1, source_target_pairs={{0,12},{4,0},{8,4},{12,8},{1,13},{5,1},{9,5},{13,9},{2,14},{6,2},{... | collective-permute-start | bytes 589832 | tf_op jit(solution)/shard_map/ppermute | solution.py:19
  219.1 36.3 %collective-permute-start.39 = (bf16[256,1536]{0,1:T(8,128)(2,1)S(1)}, bf16[256,1536]{0,1:T(8,128)(2,1)}, u32[]{:S(2)}, u32[]{:S(2)}) collective-permute-start(bf16[256,1536]{0,1:T(8,128)(2,1)S(1)} %dynamic_update_slice.119), channel_id=1, source_target_pairs={{0,4},{4,8},{8,12},{12,0},{1,5},{5,9},{9,13},{13,1},{2,6},{6,10},{... | collective-permute-start | bytes 2359304 | tf_op jit(solution)/shard_map/ppermute | solution.py:19
  219.8 38.3 %collective-permute-start.40 = (bf16[256,1536]{0,1:T(8,128)(2,1)S(1)}, bf16[256,1536]{0,1:T(8,128)(2,1)S(1)}, u32[]{:S(2)}, u32[]{:S(2)}) collective-permute-start(bf16[256,1536]{0,1:T(8,128)(2,1)S(1)} %dynamic_update_slice.119), channel_id=1, source_target_pairs={{0,8},{4,12},{8,0},{12,4},{1,9},{5,13},{9,1},{13,5},{2,10},{6,14},... | collective-permute-start | bytes 2359304 | tf_op jit(solution)/shard_map/ppermute | solution.py:19
  222.6 57.9 %collective-permute-start.1 = (f32[5,256,256]{1,2,0:T(8,128)S(1)}, f32[5,256,256]{1,2,0:T(8,128)}, u32[]{:S(2)}, u32[]{:S(2)}) collective-permute-start(f32[5,256,256]{1,2,0:T(8,128)S(1)} %dynamic-slice_add_fusion), channel_id=1, source_target_pairs={{0,2},{2,0},{1,3},{3,1},{4,6},{6,4},{5,7},{7,5},{8,10},{10,8},{9,1... | collective-permute-start | bytes 3932168 | tf_op jit(solution)/shard_map/ppermute | solution.py:19
  231.1 30.7 %collective-permute-start.41 = (bf16[256,1536]{0,1:T(8,128)(2,1)S(1)}, bf16[256,1536]{0,1:T(8,128)(2,1)}, u32[]{:S(2)}, u32[]{:S(2)}) collective-permute-start(bf16[256,1536]{0,1:T(8,128)(2,1)S(1)} %dynamic_update_slice.119), channel_id=1, source_target_pairs={{0,12},{4,0},{8,4},{12,8},{1,13},{5,1},{9,5},{13,9},{2,14},{6,2},{... | collective-permute-start | bytes 2359304 | tf_op jit(solution)/shard_map/ppermute | solution.py:19
  242.4 49.5 %collective-permute-start.52 = (bf16[256,1536]{0,1:T(8,128)(2,1)}, bf16[256,1536]{0,1:T(8,128)(2,1)}, u32[]{:S(2)}, u32[]{:S(2)}) collective-permute-start(bf16[256,1536]{0,1:T(8,128)(2,1)} %dynamic_update_slice.127), channel_id=1, source_target_pairs={{0,16},{16,32},{32,48},{48,0},{1,17},{17,33},{33,49},{49,1},{2,18}... | collective-permute-start | bytes 2359304 | tf_op jit(solution)/shard_map/ppermute | solution.py:19
  255.4 50.0 %collective-permute-start.53 = (bf16[256,1536]{0,1:T(8,128)(2,1)}, bf16[256,1536]{0,1:T(8,128)(2,1)}, u32[]{:S(2)}, u32[]{:S(2)}) collective-permute-start(bf16[256,1536]{0,1:T(8,128)(2,1)} %dynamic_update_slice.127), channel_id=1, source_target_pairs={{0,32},{16,48},{32,0},{48,16},{1,33},{17,49},{33,1},{49,17},{2,34}... | collective-permute-start | bytes 2359304 | tf_op jit(solution)/shard_map/ppermute | solution.py:19
  258.0 53.0 %collective-permute-start.54 = (bf16[256,1536]{0,1:T(8,128)(2,1)}, bf16[256,1536]{0,1:T(8,128)(2,1)}, u32[]{:S(2)}, u32[]{:S(2)}) collective-permute-start(bf16[256,1536]{0,1:T(8,128)(2,1)} %dynamic_update_slice.127), channel_id=1, source_target_pairs={{0,48},{16,0},{32,16},{48,32},{1,49},{17,1},{33,17},{49,33},{2,50}... | collective-permute-start | bytes 2359304 | tf_op jit(solution)/shard_map/ppermute | solution.py:19
  309.4 24.7 %collective-permute-start.8 = (f32[40,256]{1,0:T(8,128)S(1)}, f32[40,256]{1,0:T(8,128)}, u32[]{:S(2)}, u32[]{:S(2)}) collective-permute-start(f32[40,256]{1,0:T(8,128)S(1)} %fusion.154), channel_id=1, source_target_pairs={{0,64},{64,0},{1,65},{65,1},{2,66},{66,2},{3,67},{67,3},{4,68},{68... | collective-permute-start | bytes 122888 | tf_op jit(solution)/shard_map/ppermute | solution.py:19
  339.6 50.1 %collective-permute-start.56 = (f32[2048,256]{1,0:T(8,128)}, f32[2048,256]{1,0:T(8,128)}, u32[]{:S(2)}, u32[]{:S(2)}) collective-permute-start(f32[2048,256]{1,0:T(8,128)} %fusion.52), channel_id=1, source_target_pairs={{0,1},{1,0},{2,3},{3,2},{4,5},{5,4},{6,7},{7,6},{8,9},{9,8},{10,11... | collective-permute-start | bytes 6291464 | tf_op jit(solution)/shard_map/ppermute | solution.py:19
  389.3 332.7 %collective-permute-start.55 = (f32[2048,256]{1,0:T(8,128)}, f32[2048,256]{1,0:T(8,128)}, u32[]{:S(2)}, u32[]{:S(2)}) collective-permute-start(f32[2048,256]{1,0:T(8,128)} %fusion.55), channel_id=1, source_target_pairs={{0,1},{1,0},{2,3},{3,2},{4,5},{5,4},{6,7},{7,6},{8,9},{9,8},{10,11... | collective-permute-start | bytes 6291464 | tf_op jit(solution)/shard_map/ppermute | solution.py:19
  394.9 327.1 %collective-permute-start.57 = (f32[2048,256]{1,0:T(8,128)}, f32[2048,256]{1,0:T(8,128)}, u32[]{:S(2)}, u32[]{:S(2)}) collective-permute-start(f32[2048,256]{1,0:T(8,128)} %convolution_add_fusion.2), channel_id=1, source_target_pairs={{0,2},{2,0},{1,3},{3,1},{4,6},{6,4},{5,7},{7,5},{8,10},{10,8},{9,1... | collective-permute-start | bytes 6291464 | tf_op jit(solution)/shard_map/ppermute | solution.py:19
  728.4 48.9 %collective-permute-start.58 = (f32[2048,256]{1,0:T(8,128)S(1)}, f32[2048,256]{1,0:T(8,128)S(1)}, u32[]{:S(2)}, u32[]{:S(2)}) collective-permute-start(f32[2048,256]{1,0:T(8,128)S(1)} %fusion.10), channel_id=1, source_target_pairs={{0,2},{2,0},{1,3},{3,1},{4,6},{6,4},{5,7},{7,5},{8,10},{10,8},{9,1... | collective-permute-start | bytes 6291464 | tf_op jit(solution)/shard_map/ppermute | solution.py:19
  735.0 50.2 %collective-permute-start.59 = (f32[2048,256]{1,0:T(8,128)S(1)}, f32[2048,256]{1,0:T(8,128)S(1)}, u32[]{:S(2)}, u32[]{:S(2)}) collective-permute-start(f32[2048,256]{1,0:T(8,128)S(1)} %fusion.10), channel_id=1, source_target_pairs={{0,1},{1,0},{2,3},{3,2},{4,5},{5,4},{6,7},{7,6},{8,9},{9,8},{10,11... | collective-permute-start | bytes 6291464 | tf_op jit(solution)/shard_map/ppermute | solution.py:19
  (50 other events, 580.7 us)
